TPU v7x, 512 devices: a whole 4x8x8 slice. The times are simulated.
512 devices in a mesh: dp: 32 (over z_hi, y, core), group: 16 (over z_lo, x).
Axes of the slice: x: 4, y: 8, z: 8 (z_hi: 2, z_lo: 4; z = z_hi * 4 + z_lo), core: 2. Of those that a mesh axis runs over, the one named last changes fastest.
Arguments:
- query_rows: bfloat16 [512, 384, 768], P(('dp', 'group')), may hold values from -24 to 24, as said below
- key_rows: bfloat16 [512, 384, 768], P(('dp', 'group')), may hold values from -24 to 24, as said below
- value_rows: bfloat16 [512, 384, 768], P(('dp', 'group')), may hold values from -6 to 6
- cotangent: bfloat16 [512, 384, 768], P(('dp', 'group')), may hold values from -6 to 6
- kept_counts: int32 [512], P(('dp', 'group')), may hold values from 92 to 380, as said below
- trades: int32 [512, 2], replicated, may hold values from 0 to 1
- layer_scale: float32 [768], replicated, may hold values from 0.1 to 1
Outputs:
- attended: bfloat16 [512, 384, 768], P(('dp', 'group'))
- query_grad: bfloat16 [512, 384, 768], P(('dp', 'group'))
- key_grad: bfloat16 [512, 384, 768], P(('dp', 'group'))
- value_grad: bfloat16 [512, 384, 768], P(('dp', 'group'))
- scale_grad: float32 [768], replicated
Inputs may be any that keep to these rules, and one draw needn't show every extreme that they name: `kept_counts`: some image holds exactly 380 kept tokens. `query_rows`: entries are real numbers. `key_rows`: entries are real numbers.
All inputs are finite; a program needn't handle non-finite values.
Results may differ from a plain program's by a relative error of at most 0.025.
Values may be sent and summed in bfloat16 or wider, within the bound.
A program may use at most 64 MiB of HBM per device.

v0:
```python
import jax
import jax.numpy as jnp
from jax import lax
from jax.sharding import PartitionSpec as P

HEAD_DIM = 64


tile_rows = 128


def from_partner(value, axis, distance):
    mask = 2**distance
    pairs = [(source, source ^ mask) for source in range(lax.axis_size(axis))]
    return lax.ppermute(value, axis, pairs)


def attend_image(queries, keys, values, cotan, count, layer_scale):
    length, width = queries.shape
    heads = width // HEAD_DIM
    factor = HEAD_DIM ** (-0.5)
    total = count + 4
    tiles = (total + tile_rows - 1) // tile_rows
    keys3 = keys.reshape(length, heads, HEAD_DIM)
    values3 = values.reshape(length, heads, HEAD_DIM)
    key_valid = jnp.arange(length, dtype=jnp.int32) < total

    def tile_step(tile_index, carry):
        attended, query_grad, key_acc, value_acc, scale_part = carry
        start = tile_index * tile_rows
        query_tile = lax.dynamic_slice_in_dim(queries, start, tile_rows, 0).reshape(
            tile_rows, heads, HEAD_DIM
        )
        cotan_tile = lax.dynamic_slice_in_dim(cotan, start, tile_rows, 0).astype(jnp.float32)
        row_mask = (start + jnp.arange(tile_rows, dtype=jnp.int32) < total)[:, None]
        scores = (
            jnp.einsum("qhd,khd->hqk", query_tile, keys3, preferred_element_type=jnp.float32)
            * factor
        )
        scores = jnp.where(key_valid[None, None, :], scores, -jnp.inf)
        top = jnp.max(scores, axis=-1, keepdims=True)
        expd = jnp.exp(scores - top)
        weights = expd / jnp.sum(expd, axis=-1, keepdims=True)
        weights_low = weights.astype(jnp.bfloat16)
        mixed = jnp.einsum(
            "hqk,khd->qhd", weights_low, values3, preferred_element_type=jnp.float32
        ).astype(jnp.bfloat16)
        mixed_rows = mixed.reshape(tile_rows, width).astype(jnp.float32)
        out_tile = jnp.where(row_mask, layer_scale * mixed_rows, 0.0).astype(jnp.bfloat16)
        upstream = jnp.where(row_mask, cotan_tile * layer_scale, 0.0).astype(jnp.bfloat16)
        scale_part = scale_part + jnp.sum(jnp.where(row_mask, cotan_tile * mixed_rows, 0.0), axis=0)
        upstream3 = upstream.reshape(tile_rows, heads, HEAD_DIM)
        delta = jnp.sum(upstream3.astype(jnp.float32) * mixed.astype(jnp.float32), axis=-1)
        delta = jnp.transpose(delta, (1, 0))[..., None]
        weight_grad = jnp.einsum(
            "qhd,khd->hqk", upstream3, values3, preferred_element_type=jnp.float32
        )
        score_grad = (weights * (weight_grad - delta) * factor).astype(jnp.bfloat16)
        query_tile_grad = jnp.einsum(
            "hqk,khd->qhd", score_grad, keys3, preferred_element_type=jnp.float32
        ).astype(jnp.bfloat16)
        key_acc = key_acc + jnp.einsum(
            "hqk,qhd->khd", score_grad, query_tile, preferred_element_type=jnp.float32
        )
        value_acc = value_acc + jnp.einsum(
            "hqk,qhd->khd", weights_low, upstream3, preferred_element_type=jnp.float32
        )
        attended = lax.dynamic_update_slice_in_dim(attended, out_tile, start, 0)
        query_grad = lax.dynamic_update_slice_in_dim(
            query_grad, query_tile_grad.reshape(tile_rows, width), start, 0
        )
        return (attended, query_grad, key_acc, value_acc, scale_part)

    start_carry = (
        jnp.zeros((length, width), jnp.bfloat16),
        jnp.zeros((length, width), jnp.bfloat16),
        jnp.zeros((length, heads, HEAD_DIM), jnp.float32),
        jnp.zeros((length, heads, HEAD_DIM), jnp.float32),
        jnp.zeros((width,), jnp.float32),
    )
    attended, query_grad, key_acc, value_acc, scale_part = lax.fori_loop(
        0, tiles, tile_step, start_carry
    )
    key_grad = key_acc.reshape(length, width).astype(jnp.bfloat16)
    value_grad = value_acc.reshape(length, width).astype(jnp.bfloat16)
    return (attended, query_grad, key_grad, value_grad, scale_part)


def attend_local(query_rows, key_rows, value_rows, cotangent, kept_counts, layer_scale):
    results = [
        attend_image(
            query_rows[0], key_rows[0], value_rows[0], cotangent[0], kept_counts[0], layer_scale
        )
    ]
    stacked = [jnp.stack([item[index] for item in results], axis=0) for index in range(4)]
    scale_part = sum((item[4] for item in results))
    return (stacked[0], stacked[1], stacked[2], stacked[3], scale_part)


def take_slot(array, slot_index):
    return lax.dynamic_index_in_dim(array, slot_index, 0, keepdims=True)


def put_slot(array, piece, slot_index):
    return lax.dynamic_update_index_in_dim(array, piece, slot_index, 0)


def trade_flag(trades, device_index, flip_bit, round_index):
    lower = jnp.bitwise_and(device_index, jnp.int32(~(1 << flip_bit)))
    return trades[lower, round_index] == 1


def per_device(query_rows, key_rows, value_rows, cotangent, kept_counts, trades, layer_scale):
    group_bits = lax.axis_size("group").bit_length() - 1
    rounds = trades.shape[1]
    slots = query_rows.shape[0]
    device_index = lax.axis_index(("dp", "group"))
    moved_q, moved_k, moved_v = (query_rows, key_rows, value_rows)
    count_pair = jnp.stack([kept_counts // 64, kept_counts % 64], axis=1).astype(jnp.bfloat16)
    for round_index in range(rounds):
        flip_bit = group_bits - 1 - round_index
        slot_index = round_index % slots
        flag = trade_flag(trades, device_index, flip_bit, round_index)
        own_q, own_k, own_v, own_n = (
            take_slot(moved_q, slot_index),
            take_slot(moved_k, slot_index),
            take_slot(moved_v, slot_index),
            take_slot(count_pair, slot_index),
        )
        got_q, got_k, got_v, got_n = from_partner((own_q, own_k, own_v, own_n), "group", flip_bit)
        moved_q = put_slot(moved_q, jnp.where(flag, got_q, own_q), slot_index)
        moved_k = put_slot(moved_k, jnp.where(flag, got_k, own_k), slot_index)
        moved_v = put_slot(moved_v, jnp.where(flag, got_v, own_v), slot_index)
        count_pair = put_slot(count_pair, jnp.where(flag, got_n, own_n), slot_index)
    pair_int = count_pair.astype(jnp.int32)
    moved_n = pair_int[:, 0] * 64 + pair_int[:, 1]
    attended, query_grad, key_grad, value_grad, scale_part = attend_local(
        moved_q, moved_k, moved_v, cotangent, moved_n, layer_scale
    )
    for round_index in reversed(range(rounds)):
        flip_bit = group_bits - 1 - round_index
        slot_index = round_index % slots
        flag = trade_flag(trades, device_index, flip_bit, round_index)
        own_q, own_k, own_v = (
            take_slot(query_grad, slot_index),
            take_slot(key_grad, slot_index),
            take_slot(value_grad, slot_index),
        )
        back_q, back_k, back_v = from_partner((own_q, own_k, own_v), "group", flip_bit)
        query_grad = put_slot(query_grad, jnp.where(flag, back_q, own_q), slot_index)
        key_grad = put_slot(key_grad, jnp.where(flag, back_k, own_k), slot_index)
        value_grad = put_slot(value_grad, jnp.where(flag, back_v, own_v), slot_index)
    scale_grad = lax.psum(scale_part, ("dp", "group"))
    return (attended, query_grad, key_grad, value_grad, scale_grad)


def solution(mesh):
    return jax.shard_map(
        per_device,
        mesh=mesh,
        in_specs=(
            P(("dp", "group"), None, None),
            P(("dp", "group"), None, None),
            P(("dp", "group"), None, None),
            P(("dp", "group"), None, None),
            P(("dp", "group")),
            P(),
            P(),
        ),
        out_specs=(
            P(("dp", "group"), None, None),
            P(("dp", "group"), None, None),
            P(("dp", "group"), None, None),
            P(("dp", "group"), None, None),
            P(),
        ),
        check_vma=False,
    )
```

profile of v0, /device:TPU:1, one launch (start us, length us, event | category | flops | bytes accessed | tf_op | source)
XLA Modules:
  0.0 363.6 jit_solution(4344200197073522969)
XLA Ops:
  0.7 1.5 copy.22
  2.1 6.6 %collective-permute-start.4 = (bf16[1,384,768]{1,2,0:T(8,128)(2,1)S(1)}, bf16[1,384,768]{1,2,0:T(8,128)(2,1)S(1)}, u32[]{:S(2)}, u32[]{:S(2)}) collective-permute-start(bf16[1,384,768]{1,2,0:T(8,128)(2,1)S(1)} %copy.22), channel_id=1, source_target_pairs={{0,8},{1,9},{2,10},{3,11},{4,12},{5,13},{6,14},{7,15},{8,0},{9,1},... | collective-permute-start | bytes 1769480 | tf_op jit(solution)/shard_map/ppermute | solution.py:15
  9.5 2.0 collective-permute-start
  11.9 4.3 %collective-permute-start.6 = (bf16[1,384,768]{1,2,0:T(8,128)(2,1)S(1)}, bf16[1,384,768]{1,2,0:T(8,128)(2,1)}, u32[]{:S(2)}, u32[]{:S(2)}) collective-permute-start(bf16[1,384,768]{1,2,0:T(8,128)(2,1)S(1)} %copy.24), channel_id=1, source_target_pairs={{0,8},{1,9},{2,10},{3,11},{4,12},{5,13},{6,14},{7,15},{8,0},{9,1},... | collective-permute-start | bytes 1769480 | tf_op jit(solution)/shard_map/ppermute | solution.py:15
  16.5 1.9 collective-permute-start.2
  18.4 1.3 constant_dynamic-slice_fusion.1
  21.1 1.1 copy.26
  22.2 36.4 %collective-permute-done = bf16[1,2]{1,0:T(2,128)(2,1)S(1)} collective-permute-done((bf16[1,2]{1,0:T(2,128)(2,1)S(1)}, bf16[1,2]{1,0:T(2,128)(2,1)S(1)}, u32[]{:S(2)}, u32[]{:S(2)}) %collective-permute-start) | collective-permute-done | bytes 36 | tf_op jit(solution)/shard_map/ppermute | solution.py:15
  58.7 4.3 %collective-permute-start.1 = (bf16[1,2]{1,0:T(2,128)(2,1)S(1)}, bf16[1,2]{1,0:T(2,128)(2,1)S(1)}, u32[]{:S(2)}, u32[]{:S(2)}) collective-permute-start(bf16[1,2]{1,0:T(2,128)(2,1)S(1)} %broadcast_select_fusion.11), channel_id=1, source_target_pairs={{0,4},{1,5},{2,6},{3,7},{4,0},{5,1},{6,2},{7,3},{8,12},{9,13},{10,... | collective-permute-start | bytes 20 | tf_op jit(solution)/shard_map/ppermute | solution.py:15
  62.9 1.4 collective-permute-done.1
  64.4 2.9 collective-permute-start.5
  67.3 4.1 %collective-permute-done.6 = bf16[1,384,768]{1,2,0:T(8,128)(2,1)} collective-permute-done((bf16[1,384,768]{1,2,0:T(8,128)(2,1)S(1)}, bf16[1,384,768]{1,2,0:T(8,128)(2,1)}, u32[]{:S(2)}, u32[]{:S(2)}) %collective-permute-start.6) | collective-permute-done | bytes 589856 | tf_op jit(solution)/shard_map/ppermute | solution.py:15
  71.4 1.1 broadcast_select_fusion.3
  72.5 3.1 collective-permute-start.7
  75.6 8.4 %collective-permute-done.2 = bf16[1,384,768]{1,2,0:T(8,128)(2,1)} collective-permute-done((bf16[1,384,768]{1,2,0:T(8,128)(2,1)S(1)}, bf16[1,384,768]{1,2,0:T(8,128)(2,1)}, u32[]{:S(2)}, u32[]{:S(2)}) %collective-permute-start.2) | collective-permute-done | bytes 589856 | tf_op jit(solution)/shard_map/ppermute | solution.py:15
  84.0 1.1 broadcast_select_fusion.5
  85.2 3.1 collective-permute-start.3
  88.2 0.6 fusion.26
  90.1 8.3 %collective-permute-done.5 = bf16[1,384,768]{1,2,0:T(8,128)(2,1)S(1)} collective-permute-done((bf16[1,384,768]{1,2,0:T(8,128)(2,1)S(1)}, bf16[1,384,768]{1,2,0:T(8,128)(2,1)S(1)}, u32[]{:S(2)}, u32[]{:S(2)}) %collective-permute-start.5) | collective-permute-done | bytes 589856 | tf_op jit(solution)/shard_map/ppermute | solution.py:15
  98.5 12.7 %collective-permute-done.7 = bf16[1,384,768]{1,2,0:T(8,128)(2,1)} collective-permute-done((bf16[1,384,768]{1,2,0:T(8,128)(2,1)S(1)}, bf16[1,384,768]{1,2,0:T(8,128)(2,1)}, u32[]{:S(2)}, u32[]{:S(2)}) %collective-permute-start.7) | collective-permute-done | bytes 589856 | tf_op jit(solution)/shard_map/ppermute | solution.py:15
  111.2 0.9 broadcast_select_fusion.9
  112.1 11.6 %collective-permute-done.3 = bf16[1,384,768]{1,2,0:T(8,128)(2,1)S(1)} collective-permute-done((bf16[1,384,768]{1,2,0:T(8,128)(2,1)S(1)}, bf16[1,384,768]{1,2,0:T(8,128)(2,1)S(1)}, u32[]{:S(2)}, u32[]{:S(2)}) %collective-permute-start.3) | collective-permute-done | bytes 589856 | tf_op jit(solution)/shard_map/ppermute | solution.py:15
  123.7 0.9 select_bitcast_fusion
  124.8 0.9 broadcast.27
  125.7 0.9 broadcast.27.clone
  126.5 35.3 %while.20 = (s32[]{:T(128)}, bf16[384,768]{1,0:T(8,128)(2,1)}, bf16[384,768]{0,1:T(8,128)(2,1)}, f32[384,12,64]{0,2,1:T(8,128)S(1)}, f32[384,12,64]{0,2,1:T(8,12...) while((s32[]{:T(128)}, bf16[384,768]{1,0:T(8,128)(2,1)}, ...), condition=%wide.region_5.6_spmd.clone.clone, body=%wide.region_0.5_spmd.clone.clone.sunk | while | flops 462814720 | bytes 36426016 | solution.py:81
  126.5 0.9 constant_dynamic-slice_fusion.4
  127.5 2.3 fusion.67
  129.8 2.6 fusion.68
  132.5 1.3 fusion.69
  134.9 0.7 multiply_convert_fusion.2
  136.1 0.6 convolution_convert_fusion.3
  136.8 0.7 constant_dynamic-update-slice_fusion.5
  137.6 0.7 constant_dynamic-update-slice_fusion.4
  138.3 0.9 constant_dynamic-slice_fusion.4
  139.3 2.3 fusion.67
  141.6 2.6 fusion.68
  144.3 1.3 fusion.69
  146.6 0.7 multiply_convert_fusion.2
  147.9 0.7 convolution_convert_fusion.3
  148.5 0.7 constant_dynamic-update-slice_fusion.5
  149.4 0.7 constant_dynamic-update-slice_fusion.4
  150.1 0.9 constant_dynamic-slice_fusion.4
  151.1 2.3 fusion.67
  153.4 2.6 fusion.68
  156.1 1.3 fusion.69
  158.4 0.7 multiply_convert_fusion.2
  159.7 0.6 convolution_convert_fusion.3
  160.3 0.7 constant_dynamic-update-slice_fusion.5
  161.2 0.7 constant_dynamic-update-slice_fusion.4
  162.0 2.1 collective-permute-start.12
  164.1 3.4 collective-permute-start.10
  167.5 1.9 collective-permute-start.8
  169.4 9.0 %collective-permute-done.12 = bf16[1,384,768]{1,2,0:T(8,128)(2,1)S(1)} collective-permute-done((bf16[1,384,768]{1,2,0:T(8,128)(2,1)S(1)}, bf16[1,384,768]{1,2,0:T(8,128)(2,1)S(1)}, u32[]{:S(2)}, u32[]{:S(2)}) %collective-permute-start.12) | collective-permute-done | bytes 589856 | tf_op jit(solution)/shard_map/ppermute | solution.py:15
  178.5 4.7 %collective-permute-start.13 = (bf16[1,384,768]{1,2,0:T(8,128)(2,1)S(1)}, bf16[1,384,768]{1,2,0:T(8,128)(2,1)S(1)}, u32[]{:S(2)}, u32[]{:S(2)}) collective-permute-start(bf16[1,384,768]{1,2,0:T(8,128)(2,1)S(1)} %broadcast_select_fusion.6), channel_id=1, source_target_pairs={{0,8},{1,9},{2,10},{3,11},{4,12},{5,13},{6,14},{7,15},{8,0},{9,1},... | collective-permute-start | bytes 1769480 | tf_op jit(solution)/shard_map/ppermute | solution.py:15
  183.2 20.5 %collective-permute-done.10 = bf16[1,384,768]{1,2,0:T(8,128)(2,1)S(1)} collective-permute-done((bf16[1,384,768]{1,2,0:T(8,128)(2,1)S(1)}, bf16[1,384,768]{1,2,0:T(8,128)(2,1)S(1)}, u32[]{:S(2)}, u32[]{:S(2)}) %collective-permute-start.10) | collective-permute-done | bytes 589856 | tf_op jit(solution)/shard_map/ppermute | solution.py:15
  203.8 4.2 %collective-permute-start.11 = (bf16[1,384,768]{1,2,0:T(8,128)(2,1)S(1)}, bf16[1,384,768]{1,2,0:T(8,128)(2,1)S(1)}, u32[]{:S(2)}, u32[]{:S(2)}) collective-permute-start(bf16[1,384,768]{1,2,0:T(8,128)(2,1)S(1)} %broadcast_select_fusion.7), channel_id=1, source_target_pairs={{0,8},{1,9},{2,10},{3,11},{4,12},{5,13},{6,14},{7,15},{8,0},{9,1},... | collective-permute-start | bytes 1769480 | tf_op jit(solution)/shard_map/ppermute | solution.py:15
  208.0 8.4 %collective-permute-done.8 = bf16[1,384,768]{1,2,0:T(8,128)(2,1)S(1)} collective-permute-done((bf16[1,384,768]{1,2,0:T(8,128)(2,1)S(1)}, bf16[1,384,768]{1,2,0:T(8,128)(2,1)S(1)}, u32[]{:S(2)}, u32[]{:S(2)}) %collective-permute-start.8) | collective-permute-done | bytes 589856 | tf_op jit(solution)/shard_map/ppermute | solution.py:15
  216.5 2.6 collective-permute-start.9
  219.2 139.9 %psum.7 = f32[768]{0:T(1024)} all-reduce(f32[768]{0:T(1024)S(1)} %get-tuple-element.86), channel_id=1, replica_groups=mesh['dp'=32,'group'=16] {'dp','group'}, use_global_device_ids=true, to_apply=%region_6.7 | all-reduce | flops 768 | bytes 6144 | tf_op jit(solution)/shard_map/psum | solution.py:153
  359.1 1.1 copy.30
  360.3 1.1 copy.29
  361.4 1.1 broadcast_select_fusion.2
  362.5 1.1 copy.28
  (64 shorter events, 6.8 us)
Async XLA Ops:
  0.6 10.9 %copy-start.1 = (bf16[1,384,768]{2,1,0:T(8,128)(2,1)S(1)}, bf16[1,384,768]{2,1,0:T(8,128)(2,1)}, u32[]{:S(2)}) copy-start(bf16[1,384,768]{2,1,0:T(8,128)(2,1)} %param.11) | copy-start | bytes 1769476
  0.6 15.5 %copy-start.2 = (bf16[1,384,768]{2,1,0:T(8,128)(2,1)S(1)}, bf16[1,384,768]{2,1,0:T(8,128)(2,1)}, u32[]{:S(2)}) copy-start(bf16[1,384,768]{2,1,0:T(8,128)(2,1)} %param.9) | copy-start | bytes 1769476
  2.1 62.2 %collective-permute-start.4 = (bf16[1,384,768]{1,2,0:T(8,128)(2,1)S(1)}, bf16[1,384,768]{1,2,0:T(8,128)(2,1)S(1)}, u32[]{:S(2)}, u32[]{:S(2)}) collective-permute-start(bf16[1,384,768]{1,2,0:T(8,128)(2,1)S(1)} %copy.22), channel_id=1, source_target_pairs={{0,8},{1,9},{2,10},{3,11},{4,12},{5,13},{6,14},{7,15},{8,0},{9,1},... | collective-permute-start | bytes 1769480 | tf_op jit(solution)/shard_map/ppermute | solution.py:15
  9.5 11.6 %copy-start.3 = (bf16[1,384,768]{2,1,0:T(8,128)(2,1)S(1)}, bf16[1,384,768]{2,1,0:T(8,128)(2,1)}, u32[]{:S(2)}) copy-start(bf16[1,384,768]{2,1,0:T(8,128)(2,1)} %param.12) | copy-start | bytes 1769476
  9.5 49.1 %collective-permute-start = (bf16[1,2]{1,0:T(2,128)(2,1)S(1)}, bf16[1,2]{1,0:T(2,128)(2,1)S(1)}, u32[]{:S(2)}, u32[]{:S(2)}) collective-permute-start(bf16[1,2]{1,0:T(2,128)(2,1)S(1)} %pad_maximum_fusion), channel_id=1, source_target_pairs={{0,8},{1,9},{2,10},{3,11},{4,12},{5,13},{6,14},{7,15},{8,0},{9,1},... | collective-permute-start | bytes 20 | tf_op jit(solution)/shard_map/ppermute | solution.py:15
  11.9 59.5 %collective-permute-start.6 = (bf16[1,384,768]{1,2,0:T(8,128)(2,1)S(1)}, bf16[1,384,768]{1,2,0:T(8,128)(2,1)}, u32[]{:S(2)}, u32[]{:S(2)}) collective-permute-start(bf16[1,384,768]{1,2,0:T(8,128)(2,1)S(1)} %copy.24), channel_id=1, source_target_pairs={{0,8},{1,9},{2,10},{3,11},{4,12},{5,13},{6,14},{7,15},{8,0},{9,1},... | collective-permute-start | bytes 1769480 | tf_op jit(solution)/shard_map/ppermute | solution.py:15
  16.5 67.6 %collective-permute-start.2 = (bf16[1,384,768]{1,2,0:T(8,128)(2,1)S(1)}, bf16[1,384,768]{1,2,0:T(8,128)(2,1)}, u32[]{:S(2)}, u32[]{:S(2)}) collective-permute-start(bf16[1,384,768]{1,2,0:T(8,128)(2,1)S(1)} %copy.20), channel_id=1, source_target_pairs={{0,8},{1,9},{2,10},{3,11},{4,12},{5,13},{6,14},{7,15},{8,0},{9,1},... | collective-permute-start | bytes 1769480 | tf_op jit(solution)/shard_map/ppermute | solution.py:15
  58.7 5.6 %collective-permute-start.1 = (bf16[1,2]{1,0:T(2,128)(2,1)S(1)}, bf16[1,2]{1,0:T(2,128)(2,1)S(1)}, u32[]{:S(2)}, u32[]{:S(2)}) collective-permute-start(bf16[1,2]{1,0:T(2,128)(2,1)S(1)} %broadcast_select_fusion.11), channel_id=1, source_target_pairs={{0,4},{1,5},{2,6},{3,7},{4,0},{5,1},{6,2},{7,3},{8,12},{9,13},{10,... | collective-permute-start | bytes 20 | tf_op jit(solution)/shard_map/ppermute | solution.py:15
  64.4 34.0 %collective-permute-start.5 = (bf16[1,384,768]{1,2,0:T(8,128)(2,1)S(1)}, bf16[1,384,768]{1,2,0:T(8,128)(2,1)S(1)}, u32[]{:S(2)}, u32[]{:S(2)}) collective-permute-start(bf16[1,384,768]{1,2,0:T(8,128)(2,1)S(1)} %broadcast_select_fusion.4), channel_id=1, source_target_pairs={{0,4},{1,5},{2,6},{3,7},{4,0},{5,1},{6,2},{7,3},{8,12},{9,13},{10,... | collective-permute-start | bytes 1769480 | tf_op jit(solution)/shard_map/ppermute | solution.py:15
  72.5 38.6 %collective-permute-start.7 = (bf16[1,384,768]{1,2,0:T(8,128)(2,1)S(1)}, bf16[1,384,768]{1,2,0:T(8,128)(2,1)}, u32[]{:S(2)}, u32[]{:S(2)}) collective-permute-start(bf16[1,384,768]{1,2,0:T(8,128)(2,1)S(1)} %broadcast_select_fusion.3), channel_id=1, source_target_pairs={{0,4},{1,5},{2,6},{3,7},{4,0},{5,1},{6,2},{7,3},{8,12},{9,13},{10,... | collective-permute-start | bytes 1769480 | tf_op jit(solution)/shard_map/ppermute | solution.py:15
  85.2 38.5 %collective-permute-start.3 = (bf16[1,384,768]{1,2,0:T(8,128)(2,1)S(1)}, bf16[1,384,768]{1,2,0:T(8,128)(2,1)S(1)}, u32[]{:S(2)}, u32[]{:S(2)}) collective-permute-start(bf16[1,384,768]{1,2,0:T(8,128)(2,1)S(1)} %broadcast_select_fusion.5), channel_id=1, source_target_pairs={{0,4},{1,5},{2,6},{3,7},{4,0},{5,1},{6,2},{7,3},{8,12},{9,13},{10,... | collective-permute-start | bytes 1769480 | tf_op jit(solution)/shard_map/ppermute | solution.py:15
  124.7 1.8 copy-start.5
  129.8 4.0 %copy-start.6 = (f32[12,128,384]{2,1,0:T(8,128)S(1)}, f32[12,128,384]{2,1,0:T(8,128)}, u32[]{:S(2)}) copy-start(f32[12,128,384]{2,1,0:T(8,128)} %get-tuple-element.288) | copy-start | bytes 7077892 | tf_op jit(solution)/shard_map/while
  133.8 1.1 copy-start.4
  141.6 4.0 %copy-start.6 = (f32[12,128,384]{2,1,0:T(8,128)S(1)}, f32[12,128,384]{2,1,0:T(8,128)}, u32[]{:S(2)}) copy-start(f32[12,128,384]{2,1,0:T(8,128)} %get-tuple-element.288) | copy-start | bytes 7077892 | tf_op jit(solution)/shard_map/while
  145.6 1.1 copy-start.4
  153.4 4.0 %copy-start.6 = (f32[12,128,384]{2,1,0:T(8,128)S(1)}, f32[12,128,384]{2,1,0:T(8,128)}, u32[]{:S(2)}) copy-start(f32[12,128,384]{2,1,0:T(8,128)} %get-tuple-element.288) | copy-start | bytes 7077892 | tf_op jit(solution)/shard_map/while
  157.4 1.1 copy-start.4
  162.0 5.5 %copy-start = (bf16[384,768]{0,1:T(8,128)(2,1)S(1)}, bf16[384,768]{0,1:T(8,128)(2,1)}, u32[]{:S(2)}) copy-start(bf16[384,768]{0,1:T(8,128)(2,1)} %get-tuple-element.83) | copy-start | bytes 1769476
  162.0 16.4 %collective-permute-start.12 = (bf16[1,384,768]{1,2,0:T(8,128)(2,1)S(1)}, bf16[1,384,768]{1,2,0:T(8,128)(2,1)S(1)}, u32[]{:S(2)}, u32[]{:S(2)}) collective-permute-start(bf16[1,384,768]{1,2,0:T(8,128)(2,1)S(1)} %bitcast.100), channel_id=1, source_target_pairs={{0,4},{1,5},{2,6},{3,7},{4,0},{5,1},{6,2},{7,3},{8,12},{9,13},{10,... | collective-permute-start | bytes 1769480 | tf_op jit(solution)/shard_map/ppermute | solution.py:15
  164.1 39.6 %collective-permute-start.10 = (bf16[1,384,768]{1,2,0:T(8,128)(2,1)S(1)}, bf16[1,384,768]{1,2,0:T(8,128)(2,1)S(1)}, u32[]{:S(2)}, u32[]{:S(2)}) collective-permute-start(bf16[1,384,768]{1,2,0:T(8,128)(2,1)S(1)} %bitcast.99), channel_id=1, source_target_pairs={{0,4},{1,5},{2,6},{3,7},{4,0},{5,1},{6,2},{7,3},{8,12},{9,13},{10,... | collective-permute-start | bytes 1769480 | tf_op jit(solution)/shard_map/ppermute | solution.py:15
  167.5 48.9 %collective-permute-start.8 = (bf16[1,384,768]{1,2,0:T(8,128)(2,1)S(1)}, bf16[1,384,768]{1,2,0:T(8,128)(2,1)S(1)}, u32[]{:S(2)}, u32[]{:S(2)}) collective-permute-start(bf16[1,384,768]{1,2,0:T(8,128)(2,1)S(1)} %bitcast.98), channel_id=1, source_target_pairs={{0,4},{1,5},{2,6},{3,7},{4,0},{5,1},{6,2},{7,3},{8,12},{9,13},{10,... | collective-permute-start | bytes 1769480 | tf_op jit(solution)/shard_map/ppermute | solution.py:15
  178.5 180.6 %collective-permute-start.13 = (bf16[1,384,768]{1,2,0:T(8,128)(2,1)S(1)}, bf16[1,384,768]{1,2,0:T(8,128)(2,1)S(1)}, u32[]{:S(2)}, u32[]{:S(2)}) collective-permute-start(bf16[1,384,768]{1,2,0:T(8,128)(2,1)S(1)} %broadcast_select_fusion.6), channel_id=1, source_target_pairs={{0,8},{1,9},{2,10},{3,11},{4,12},{5,13},{6,14},{7,15},{8,0},{9,1},... | collective-permute-start | bytes 1769480 | tf_op jit(solution)/shard_map/ppermute | solution.py:15
  203.8 156.4 %collective-permute-start.11 = (bf16[1,384,768]{1,2,0:T(8,128)(2,1)S(1)}, bf16[1,384,768]{1,2,0:T(8,128)(2,1)S(1)}, u32[]{:S(2)}, u32[]{:S(2)}) collective-permute-start(bf16[1,384,768]{1,2,0:T(8,128)(2,1)S(1)} %broadcast_select_fusion.7), channel_id=1, source_target_pairs={{0,8},{1,9},{2,10},{3,11},{4,12},{5,13},{6,14},{7,15},{8,0},{9,1},... | collective-permute-start | bytes 1769480 | tf_op jit(solution)/shard_map/ppermute | solution.py:15
  216.5 144.9 %collective-permute-start.9 = (bf16[1,384,768]{1,2,0:T(8,128)(2,1)S(1)}, bf16[1,384,768]{1,2,0:T(8,128)(2,1)}, u32[]{:S(2)}, u32[]{:S(2)}) collective-permute-start(bf16[1,384,768]{1,2,0:T(8,128)(2,1)S(1)} %broadcast_select_fusion.8), channel_id=1, source_target_pairs={{0,8},{1,9},{2,10},{3,11},{4,12},{5,13},{6,14},{7,15},{8,0},{9,1},... | collective-permute-start | bytes 1769480 | tf_op jit(solution)/shard_map/ppermute | solution.py:15
where the time goes:
time: 365 us; the launch traced here: 364 us
  blocking collectives  140 us (38%)
  waiting for transfers between devices  121 us (33%)
  starting transfers between devices  47.1 us (13%)
  matrix products  22.3 us (6%)
  local copies, waits for them, and re-layouts  18.9 us (5%)
  other arithmetic  10.1 us (3%)
  between operations  4.23 us (1%)
    psum x1, blocking collectives, per_device(): scale_grad = lax.psum(scale_part, ('dp', 'group'))  140 us
    ppermute x14, waiting for transfers between devices, from_partner(): return lax.ppermute(value, axis, pairs)  121 us
    ppermute x14, starting transfers between devices, from_partner(): return lax.ppermute(value, axis, pairs)  47.1 us
    dot_general x3, matrix products, tile_step(): jnp.einsum('hqk,khd->qhd', weights_low, values3, preferred_element_type=j...  7.9 us
  transfers between devices with their start and end apart: 14, of which 10 were waited for; matrix products, arithmetic and copies ran while one was open for 3% of the time, Pallas kernels for 0%

commit v1 on v0

v1 whole, which is shorter than its diff:
```python
import functools
import math

import jax
import jax.numpy as jnp
from jax import lax
from jax.experimental import pallas as pl
from jax.experimental.pallas import tpu as pltpu
from jax.sharding import PartitionSpec as P

MESH = pl.DeviceIdType.MESH
BF16 = jnp.bfloat16
F32 = jnp.float32
HEAD_DIM = 64
LANES = 128
FACTOR = HEAD_DIM ** -0.5
EXP_SCALE = FACTOR * math.log2(math.e)
PARTS = 3

NEAR, FAR = 4, 8


def flip(index, bit):
    return index + bit * (1 - 2 * ((index // bit) % 2))


def nt_dot(a, b):
    return lax.dot_general(a, b, (((1,), (1,)), ((), ())), preferred_element_type=F32)


def tn_dot(a, b):
    return lax.dot_general(a, b, (((0,), (0,)), ((), ())), preferred_element_type=F32)


def nn_dot(a, b):
    return jnp.dot(a, b, preferred_element_type=F32)


def sum_stages(dp_size):
    bits = [("group", 4), ("group", 8), ("group", 1), ("group", 2)]
    bit = 1
    while bit < dp_size:
        bits.append(("dp", bit))
        bit *= 2
    return [bits[i : i + 2] for i in range(0, len(bits), 2)]


def kernel(
    stages,
    q_hbm, k_hbm, v_hbm, c_hbm, count_ref, trades_ref, scale_ref,
    att_out, dq_out, dk_out, dv_out, sum_out,
    q, k, v, own_c, c_first, c_send, c_second, cot,
    att, a_first, a_send, a_second, att_final,
    weights, mixed, dq, dk, dv, part, sum_recv,
    load_sem, store_sem, send_sem, recv_sem, sum_send_sem, sum_recv_sem,
):
    g = lax.axis_index("group")
    d = lax.axis_index("dp")
    length, width = q.shape
    pairs = width // LANES
    half = length // 2
    rows = half // PARTS

    def peer(moves):
        pg, pd = g, d
        for axis, bit in moves:
            if axis == "group":
                pg = flip(pg, bit)
            else:
                pd = flip(pd, bit)
        return (pd, pg)

    def stage_peers(stage):
        if len(stage) == 1:
            return [[stage[0]]]
        return [[stage[0]], [stage[1]], [stage[0], stage[1]]]

    barrier = pltpu.get_barrier_semaphore()
    greeted = 0
    for stage in stages:
        for moves in stage_peers(stage):
            pl.semaphore_signal(barrier, inc=1, device_id=peer(moves), device_id_type=MESH)
            greeted += 1
    loads = [
        pltpu.make_async_copy(src.at[0], dst, load_sem.at[i])
        for i, (src, dst) in enumerate([(q_hbm, q), (k_hbm, k), (v_hbm, v), (c_hbm, own_c)])
    ]
    for copy in loads:
        copy.start()
    pl.semaphore_wait(barrier, greeted)

    a, b, x = g // 8, (g // 4) % 2, g % 4
    base = d * 16 + x

    def flag(offset, round_index):
        return trades_ref[round_index, base + offset] == 1

    far_mine, far_other = flag(b * 4, 0), flag((1 - b) * 4, 0)
    near_mine, near_other = flag(a * 8, 1), flag((1 - a) * 8, 1)
    near_at_source = jnp.logical_or(
        jnp.logical_and(far_mine, near_other),
        jnp.logical_and(jnp.logical_not(far_mine), near_mine),
    )
    far_at_source = jnp.logical_or(
        jnp.logical_and(near_mine, far_other),
        jnp.logical_and(jnp.logical_not(near_mine), far_mine),
    )

    def spans(part_index):
        return pl.ds(part_index * rows, rows), pl.ds(half + part_index * rows, rows)

    def remote(src, dst, bit, slot):
        return pltpu.make_async_remote_copy(
            src_ref=src, dst_ref=dst, send_sem=send_sem.at[slot], recv_sem=recv_sem.at[slot],
            device_id=peer([("group", bit)]), device_id_type=MESH,
        )

    c_hop1, c_hop2, a_hop1, a_hop2 = [], [], [], []
    for i in range(PARTS):
        top, low = spans(i)
        c_hop1.append((
            remote(c_hbm.at[0, top], c_first.at[top], NEAR, 8 * i),
            remote(c_hbm.at[0, low], c_first.at[low], FAR, 8 * i + 1),
        ))
        c_hop2.append((
            remote(c_send.at[top], c_second.at[top], FAR, 8 * i + 2),
            remote(c_send.at[low], c_second.at[low], NEAR, 8 * i + 3),
        ))
        a_hop1.append((
            remote(att.at[top], a_first.at[top], FAR, 8 * i + 4),
            remote(att.at[low], a_first.at[low], NEAR, 8 * i + 5),
        ))
        a_hop2.append((
            remote(a_send.at[top], a_second.at[top], NEAR, 8 * i + 6),
            remote(a_send.at[low], a_second.at[low], FAR, 8 * i + 7),
        ))

    def start(hop):
        for copy in hop:
            copy.start()

    def pick(chosen, other, pred):
        return lax.select(pred, chosen, other)

    def c_turn(i):
        top, low = spans(i)
        c_hop1[i][0].wait_recv()
        c_send[top] = pick(c_first[top], own_c[top], near_mine)
        c_hop2[i][0].start()
        c_hop1[i][1].wait_recv()
        c_send[low] = pick(c_first[low], own_c[low], far_other)
        c_hop2[i][1].start()

    def c_land(i):
        top, low = spans(i)
        c_hop2[i][0].wait_recv()
        cot[top] = pick(c_second[top], c_send[top], far_mine)
        c_hop2[i][1].wait_recv()
        cot[low] = pick(c_second[low], pick(c_first[low], own_c[low], far_mine), near_at_source)

    def a_turn(i):
        top, low = spans(i)
        a_hop1[i][0].wait_recv()
        a_send[top] = pick(a_first[top], att[top], far_mine)
        a_hop2[i][0].start()
        a_hop1[i][1].wait_recv()
        a_send[low] = pick(a_first[low], att[low], near_other)
        a_hop2[i][1].start()

    def a_store(i, which):
        span = spans(i)[which]
        return pltpu.make_async_copy(
            att_final.at[span], att_out.at[0, span], store_sem.at[3 + 2 * i + which]
        )

    def a_land(i):
        top, low = spans(i)
        a_hop2[i][0].wait_recv()
        att_final[top] = pick(a_second[top], a_send[top], near_mine)
        a_store(i, 0).start()
        a_hop2[i][1].wait_recv()
        att_final[low] = pick(a_second[low], pick(a_first[low], att[low], near_mine), far_at_source)
        a_store(i, 1).start()

    def sum_copies(s):
        return [
            pltpu.make_async_remote_copy(
                src_ref=part.at[s], dst_ref=sum_recv.at[s, j],
                send_sem=sum_send_sem.at[3 * s + j], recv_sem=sum_recv_sem.at[3 * s + j],
                device_id=peer(moves), device_id_type=MESH,
            )
            for j, moves in enumerate(stage_peers(stages[s]))
        ]

    def sum_start(s):
        for copy in sum_copies(s):
            copy.start()

    def sum_finish(s):
        for copy in sum_copies(s):
            copy.wait_recv()
        total = part[s] + sum_recv[s, 0]
        if len(stages[s]) == 2:
            total = total + (sum_recv[s, 1] + sum_recv[s, 2])
        if s + 1 < len(stages):
            part[s + 1] = total
            sum_start(s + 1)
        else:
            sum_out[...] = total

    total_rows = count_ref[0] + 4
    key_bias = jnp.where(
        lax.broadcasted_iota(jnp.int32, (1, length), 1) < total_rows, 0.0, -jnp.inf
    ).astype(F32)

    def columns(pair):
        return pl.ds(pl.multiple_of(pair * LANES, LANES), LANES)

    def halves(block):
        lane = lax.broadcasted_iota(jnp.int32, block.shape, 1)
        wide = block.astype(F32)
        return (
            jnp.where(lane < HEAD_DIM, wide, 0.0).astype(BF16),
            jnp.where(lane < HEAD_DIM, 0.0, wide).astype(BF16),
        )

    def row_valid():
        return lax.broadcasted_iota(jnp.int32, (length, LANES), 0) < total_rows

    def forward(pair, carry):
        cols = columns(pair)
        keys = k[:, cols]
        blend = None
        for j, (q_half, v_half) in enumerate(zip(halves(q[:, cols]), halves(v[:, cols]))):
            scores = nt_dot(q_half, keys) + key_bias
            top = jnp.max(scores, axis=1, keepdims=True)
            expd = jnp.exp2((scores - top) * EXP_SCALE)
            low = (expd * (1.0 / jnp.sum(expd, axis=1, keepdims=True))).astype(BF16)
            weights[2 * pair + j] = low
            term = nn_dot(low, v_half)
            blend = term if blend is None else blend + term
        mixed_low = blend.astype(BF16)
        mixed[:, cols] = mixed_low
        out = jnp.where(row_valid(), scale_ref[:, cols] * mixed_low.astype(F32), 0.0)
        att[:, cols] = out.astype(BF16)
        return carry

    def scale_part():
        part[0] = jnp.zeros((8, LANES), F32)
        for pair in range(pairs):
            cols = pl.ds(pair * LANES, LANES)
            product = cot[:, cols].astype(F32) * mixed[:, cols].astype(F32)
            part[0, pl.ds(pair, 1), :] = jnp.sum(
                jnp.where(row_valid(), product, 0.0), axis=0, keepdims=True
            )

    def backward(pair, carry):
        cols = columns(pair)
        up = jnp.where(row_valid(), cot[:, cols].astype(F32) * scale_ref[:, cols], 0.0)
        values = v[:, cols]
        blended = mixed[:, cols].astype(F32)
        dq_sum = dk_sum = dv_sum = None
        parts = zip(halves(up), halves(k[:, cols]), halves(q[:, cols]))
        for j, (up_half, k_half, q_half) in enumerate(parts):
            low = weights[2 * pair + j]
            delta = jnp.sum(up_half.astype(F32) * blended, axis=1, keepdims=True)
            grad = (low.astype(F32) * (nt_dot(up_half, values) - delta)).astype(BF16)
            dq_term, dk_term, dv_term = nn_dot(grad, k_half), tn_dot(grad, q_half), tn_dot(low, up_half)
            dq_sum = dq_term if j == 0 else dq_sum + dq_term
            dk_sum = dk_term if j == 0 else dk_sum + dk_term
            dv_sum = dv_term if j == 0 else dv_sum + dv_term
        dq[:, cols] = (dq_sum * FACTOR).astype(BF16)
        dk[:, cols] = (dk_sum * FACTOR).astype(BF16)
        dv[:, cols] = dv_sum.astype(BF16)
        return carry

    for i in range(PARTS):
        start(c_hop1[i])
    for copy in loads:
        copy.wait()
    lax.fori_loop(0, pairs // 2, forward, 0)
    c_turn(0)
    lax.fori_loop(pairs // 2, pairs, forward, 0)
    c_turn(1)
    c_turn(2)
    start(a_hop1[0])
    c_land(0)
    start(a_hop1[1])
    c_land(1)
    start(a_hop1[2])
    c_land(2)
    scale_part()
    sum_start(0)
    lax.fori_loop(0, pairs // 2, backward, 0)
    a_turn(0)
    sum_finish(0)
    lax.fori_loop(pairs // 2, pairs, backward, 0)
    grad_stores = [
        pltpu.make_async_copy(src, dst.at[0], store_sem.at[i])
        for i, (src, dst) in enumerate([(dq, dq_out), (dk, dk_out), (dv, dv_out)])
    ]
    for copy in grad_stores:
        copy.start()
    sum_finish(1)
    a_turn(1)
    sum_finish(2)
    a_turn(2)
    for s in range(3, len(stages)):
        sum_finish(s)
    for i in range(PARTS):
        a_land(i)
    for copy in grad_stores:
        copy.wait()
    for i in range(PARTS):
        for hop in (c_hop1[i], c_hop2[i], a_hop1[i], a_hop2[i]):
            for copy in hop:
                copy.wait_send()
        a_store(i, 0).wait()
        a_store(i, 1).wait()
    for s in range(len(stages)):
        for copy in sum_copies(s):
            copy.wait_send()


def per_device(stages, query_rows, key_rows, value_rows, cotangent, kept_counts, trades, layer_scale):
    _, length, width = query_rows.shape
    heads = width // HEAD_DIM
    image = jax.ShapeDtypeStruct(query_rows.shape, BF16)
    block = pltpu.VMEM((length, width), BF16)
    hbm = pl.BlockSpec(memory_space=pl.ANY)
    smem = pl.BlockSpec(memory_space=pltpu.SMEM)
    vmem = pl.BlockSpec(memory_space=pltpu.VMEM)
    slots = 8 * PARTS
    attended, query_grad, key_grad, value_grad, scale_sum = pl.pallas_call(
        functools.partial(kernel, stages),
        out_shape=(image, image, image, image, jax.ShapeDtypeStruct((8, LANES), F32)),
        in_specs=[hbm, hbm, hbm, hbm, smem, smem, vmem],
        out_specs=(hbm, hbm, hbm, hbm, vmem),
        scratch_shapes=[
            *[block] * 13,
            pltpu.VMEM((heads, length, length), BF16),
            *[block] * 4,
            pltpu.VMEM((len(stages), 8, LANES), F32),
            pltpu.VMEM((len(stages), 3, 8, LANES), F32),
            pltpu.SemaphoreType.DMA((4,)),
            pltpu.SemaphoreType.DMA((3 + 2 * PARTS,)),
            pltpu.SemaphoreType.DMA((slots,)),
            pltpu.SemaphoreType.DMA((slots,)),
            pltpu.SemaphoreType.DMA((3 * len(stages),)),
            pltpu.SemaphoreType.DMA((3 * len(stages),)),
        ],
        compiler_params=pltpu.CompilerParams(
            collective_id=0, has_side_effects=True, vmem_limit_bytes=60 * 2**20
        ),
        cost_estimate=pl.CostEstimate(
            flops=12 * heads * length * length * HEAD_DIM,
            bytes_accessed=16 * length * width,
            transcendentals=heads * length * length,
        ),
    )(
        query_rows, key_rows, value_rows, cotangent,
        kept_counts, trades.T, layer_scale.reshape(1, width),
    )
    scale_grad = scale_sum[: width // LANES].reshape(width)
    return attended, query_grad, key_grad, value_grad, scale_grad


def solution(mesh):
    rows = P(("dp", "group"), None, None)
    return jax.shard_map(
        functools.partial(per_device, sum_stages(mesh.shape["dp"])),
        mesh=mesh,
        in_specs=(rows, rows, rows, rows, P(("dp", "group")), P(), P()),
        out_specs=(rows, rows, rows, rows, P()),
        check_vma=False,
    )
```

time: 365 us -> 84.8 us (0.23)
  blocking collectives: 140 us -> 0 us
  waiting for transfers between devices: 121 us -> 0 us
  Pallas kernels: 0 us -> 75.2 us
  starting transfers between devices: 47.1 us -> 0 us
  matrix products: 22.3 us -> 0 us
  local copies, waits for them, and re-layouts: 18.9 us -> 7.88 us
  other arithmetic: 10.1 us -> 0 us
    psum x1 -> x0, blocking collectives: 140 us -> none  [per_device(): scale_grad = lax.psum(scale_part, ('dp', 'group'))]
    ppermute x14 -> x0, waiting for transfers between devices: 121 us -> none  [from_partner(): return lax.ppermute(value, axis, pairs)]
    pallas_call x0 -> x1, Pallas kernels: none -> 75.2 us  [per_device(): pl.pallas_call(functools.partial(kernel, stages), out_shape=(image, image...]
    ppermute x14 -> x0, starting transfers between devices: 47.1 us -> none  [from_partner(): return lax.ppermute(value, axis, pairs)]
    dot_general x15 -> x0, matrix products: 15.3 us -> none  [the longest x3 7.9 us: tile_step(): jnp.einsum('hqk,khd->qhd', weights_low, values3, preferred_element_type=j...]
    sub x3 -> x0, matrix products: 7.02 us -> none  [tile_step(): expd = jnp.exp(scores - top)]
    select_n x12 -> x0, other arithmetic: 4.91 us -> none  [the longest x2 2.03 us: per_device(): moved_v = put_slot(moved_v, jnp.where(flag, got_v, own_v), slot_index)]
    dynamic_update_slice x9 -> x0, local copies, waits for them, and re-layouts: 4.62 us -> none  [the longest x6 2.52 us: tile_step(): attended = lax.dynamic_update_slice_in_dim(attended, out_tile, start, 0)]
  transfers between devices with their start and end apart: 14 -> 0, of which waited for: 10 -> 0; matrix products, arithmetic and copies ran while one was open for 3% -> 0% of each run, Pallas kernels for 0% -> 0%
where the time goes in v1:
time: 84.8 us; the launch traced here: 84.4 us
  Pallas kernels  75.2 us (89%)
  local copies, waits for them, and re-layouts  7.88 us (9%)
  between operations  1.3 us (2%)
    pallas_call x1, Pallas kernels, per_device(): pl.pallas_call(functools.partial(kernel, stages), out_shape=(image, image...  75.2 us
    unnamed x12, local copies, waits for them, and re-layouts  6.02 us

profile of v1, /device:TPU:1, one launch (start us, length us, event | category | flops | bytes accessed | tf_op | source)
XLA Modules:
  0.0 84.4 jit_solution(16340491216614631196)
XLA Ops:
  1.3 1.3 %reshape.16.scale_ref = f32[1,768]{1,0:T(1,128)} reshape(f32[768]{0:T(1024)} %param.13) | data formatting | bytes 6144 | tf_op jit(solution)/shard_map/reshape | solution.py:362
  2.5 75.2 %shard_map.110 = (bf16[1,384,768]{2,1,0:T(8,128)(2,1)}, bf16[1,384,768]{2,1,0:T(8,128)(2,1)}, bf16[1,384,768]{2,1,0:T(8,128)(2,1)}, bf16[1,384,768]{2,1,0:T(8,128)(2,1)}, f32[8,128]{1,0:T(8,128)}) custom-call(bf16[1,384,768]{2,1,0:T(8,128)(2,1)} %q_hbm.1, bf16[1,384,768]{2,1,0:T(8,128)(2,1)} %k_hbm.1, bf16[1,384,768]{2,1,0:T(8,128)(2,1)} %v_hbm.1, ...), custom_call_target="tpu_custom_call" | custom-call | flops 1358954496 | bytes 4718592 | tf_op jit(solution)/shard_map/pallas_call | solution.py:334
  77.8 0.0 copy-start.3
  77.8 0.7 copy-done.3
  78.4 0.6 slice_bitcast_fusion
  79.0 0.0 copy-start.2
  79.0 2.0 %copy.17 = bf16[1,384,768]{2,1,0:T(8,128)(2,1)} copy(bf16[1,384,768]{2,1,0:T(8,128)(2,1)} %get-tuple-element.20) | data formatting | bytes 1179648
  81.0 0.0 copy-done.2
  81.0 0.0 copy-start.1
  81.0 0.8 copy.18
  81.8 0.5 copy-done.1
  82.3 0.0 copy-start
  82.3 0.8 copy.19
  83.1 0.5 copy-done
  83.6 0.8 copy.20
Async XLA Ops:
  77.8 0.7 copy-start.3
  79.0 2.0 %copy-start.2 = (bf16[1,384,768]{2,1,0:T(8,128)(2,1)S(1)}, bf16[1,384,768]{2,1,0:T(8,128)(2,1)}, u32[]{:S(2)}) copy-start(bf16[1,384,768]{2,1,0:T(8,128)(2,1)} %get-tuple-element.21) | copy-start | bytes 1769476
  81.0 1.3 %copy-start.1 = (bf16[1,384,768]{2,1,0:T(8,128)(2,1)S(1)}, bf16[1,384,768]{2,1,0:T(8,128)(2,1)}, u32[]{:S(2)}) copy-start(bf16[1,384,768]{2,1,0:T(8,128)(2,1)} %get-tuple-element.22) | copy-start | bytes 1769476
  82.3 1.3 %copy-start = (bf16[1,384,768]{2,1,0:T(8,128)(2,1)S(1)}, bf16[1,384,768]{2,1,0:T(8,128)(2,1)}, u32[]{:S(2)}) copy-start(bf16[1,384,768]{2,1,0:T(8,128)(2,1)} %get-tuple-element.23) | copy-start | bytes 1769476

commit v2 on v1

--- a/solution.py
+++ b/solution.py
@@ -37,22 +37,33 @@
 
 
 def sum_stages(dp_size):
-    bits = [("group", 4), ("group", 8), ("group", 1), ("group", 2)]
-    bit = 1
-    while bit < dp_size:
-        bits.append(("dp", bit))
+    top = dp_size // 2
+    middle, bit = [], 2
+    while bit < top:
+        middle.insert(0, ("dp", bit))
         bit *= 2
-    return [bits[i : i + 2] for i in range(0, len(bits), 2)]
+    stages = [
+        [("group", 2), ("group", 1), ("dp", 1)], middle, [("dp", top), ("group", FAR), ("group", NEAR)]
+    ]
+    return [stage for stage in stages if stage]
+
+
+def stage_moves(stage):
+    count = len(stage)
+    return [
+        [stage[i] for i in range(count) if choice >> (count - 1 - i) & 1]
+        for choice in range(1, 2**count)
+    ]
 
 
 def kernel(
     stages,
-    q_hbm, k_hbm, v_hbm, c_hbm, count_ref, trades_ref, scale_ref,
-    att_out, dq_out, dk_out, dv_out, sum_out,
+    q_hbm, k_hbm, v_hbm, c_hbm, count_hbm, trades_hbm, scale_hbm,
+    att_final, dq, dk, dv, sum_out,
     q, k, v, own_c, c_first, c_send, c_second, cot,
-    att, a_first, a_send, a_second, att_final,
-    weights, mixed, dq, dk, dv, part, sum_recv,
-    load_sem, store_sem, send_sem, recv_sem, sum_send_sem, sum_recv_sem,
+    att, a_first, a_send, a_second,
+    weights, mixed, part, sum_recv, scale_ref, count_ref, trades_ref,
+    load_sem, send_sem, recv_sem, sum_send_sem, sum_recv_sem, ready,
 ):
     g = lax.axis_index("group")
     d = lax.axis_index("dp")
@@ -70,41 +81,51 @@
                 pd = flip(pd, bit)
         return (pd, pg)
 
-    def stage_peers(stage):
-        if len(stage) == 1:
-            return [[stage[0]]]
-        return [[stage[0]], [stage[1]], [stage[0], stage[1]]]
-
-    barrier = pltpu.get_barrier_semaphore()
-    greeted = 0
-    for stage in stages:
-        for moves in stage_peers(stage):
-            pl.semaphore_signal(barrier, inc=1, device_id=peer(moves), device_id_type=MESH)
-            greeted += 1
+    def upper(moves):
+        axis, bit = moves[0]
+        return ((g if axis == "group" else d) // bit) % 2
+
     loads = [
-        pltpu.make_async_copy(src.at[0], dst, load_sem.at[i])
-        for i, (src, dst) in enumerate([(q_hbm, q), (k_hbm, k), (v_hbm, v), (c_hbm, own_c)])
+        pltpu.make_async_copy(src, dst, load_sem.at[i])
+        for i, (src, dst) in enumerate([
+            (q_hbm.at[0], q), (k_hbm.at[0], k), (v_hbm.at[0], v), (c_hbm.at[0], own_c),
+            (count_hbm, count_ref), (trades_hbm, trades_ref), (scale_hbm, scale_ref),
+        ])
     ]
     for copy in loads:
         copy.start()
-    pl.semaphore_wait(barrier, greeted)
-
-    a, b, x = g // 8, (g // 4) % 2, g % 4
-    base = d * 16 + x
-
-    def flag(offset, round_index):
-        return trades_ref[round_index, base + offset] == 1
-
-    far_mine, far_other = flag(b * 4, 0), flag((1 - b) * 4, 0)
-    near_mine, near_other = flag(a * 8, 1), flag((1 - a) * 8, 1)
-    near_at_source = jnp.logical_or(
-        jnp.logical_and(far_mine, near_other),
-        jnp.logical_and(jnp.logical_not(far_mine), near_mine),
-    )
-    far_at_source = jnp.logical_or(
-        jnp.logical_and(near_mine, far_other),
-        jnp.logical_and(jnp.logical_not(near_mine), far_mine),
-    )
+
+    meetings = [moves for stage in stages for moves in stage_moves(stage)]
+    barrier = pltpu.get_barrier_semaphore()
+    greetings = 0
+    for moves in meetings:
+        greetings = greetings + upper(moves)
+
+        @pl.when(upper(moves) == 0)
+        def _(moves=moves):
+            pl.semaphore_signal(barrier, inc=1, device_id=peer(moves), device_id_type=MESH)
+
+    @pl.when(greetings > 0)
+    def _():
+        pl.semaphore_wait(barrier, greetings)
+
+    for j, moves in enumerate(meetings):
+
+        @pl.when(upper(moves) == 1)
+        def _(j=j, moves=moves):
+            pl.semaphore_signal(ready.at[j], inc=1, device_id=peer(moves), device_id_type=MESH)
+
+    met = []
+
+    def meet(moves):
+        j = meetings.index(moves)
+        if j in met:
+            return
+        met.append(j)
+
+        @pl.when(upper(moves) == 0)
+        def _():
+            pl.semaphore_wait(ready.at[j], 1)
 
     def spans(part_index):
         return pl.ds(part_index * rows, rows), pl.ds(half + part_index * rows, rows)
@@ -167,46 +188,66 @@
         a_send[low] = pick(a_first[low], att[low], near_other)
         a_hop2[i][1].start()
 
-    def a_store(i, which):
-        span = spans(i)[which]
-        return pltpu.make_async_copy(
-            att_final.at[span], att_out.at[0, span], store_sem.at[3 + 2 * i + which]
-        )
-
     def a_land(i):
         top, low = spans(i)
         a_hop2[i][0].wait_recv()
-        att_final[top] = pick(a_second[top], a_send[top], near_mine)
-        a_store(i, 0).start()
+        att_final[0, top] = pick(a_second[top], a_send[top], near_mine)
         a_hop2[i][1].wait_recv()
-        att_final[low] = pick(a_second[low], pick(a_first[low], att[low], near_mine), far_at_source)
-        a_store(i, 1).start()
+        att_final[0, low] = pick(a_second[low], pick(a_first[low], att[low], near_mine), far_at_source)
 
     def sum_copies(s):
         return [
             pltpu.make_async_remote_copy(
                 src_ref=part.at[s], dst_ref=sum_recv.at[s, j],
-                send_sem=sum_send_sem.at[3 * s + j], recv_sem=sum_recv_sem.at[3 * s + j],
+                send_sem=sum_send_sem.at[7 * s + j], recv_sem=sum_recv_sem.at[7 * s + j],
                 device_id=peer(moves), device_id_type=MESH,
             )
-            for j, moves in enumerate(stage_peers(stages[s]))
+            for j, moves in enumerate(stage_moves(stages[s]))
         ]
 
     def sum_start(s):
+        for moves in stage_moves(stages[s]):
+            meet(moves)
         for copy in sum_copies(s):
             copy.start()
 
     def sum_finish(s):
         for copy in sum_copies(s):
             copy.wait_recv()
-        total = part[s] + sum_recv[s, 0]
-        if len(stages[s]) == 2:
-            total = total + (sum_recv[s, 1] + sum_recv[s, 2])
+        terms = [part[s]] + [sum_recv[s, j] for j in range(len(stage_moves(stages[s])))]
+        while len(terms) > 1:
+            terms = [terms[i] + terms[i + 1] for i in range(0, len(terms), 2)]
         if s + 1 < len(stages):
-            part[s + 1] = total
+            part[s + 1] = terms[0]
             sum_start(s + 1)
         else:
-            sum_out[...] = total
+            sum_out[...] = terms[0][: width // LANES]
+
+    start_near = [c_hop1[i][0] for i in range(PARTS)]
+    start_far = [c_hop1[i][1] for i in range(PARTS)]
+    meet([("group", NEAR)])
+    start(start_near)
+    meet([("group", FAR)])
+    start(start_far)
+    for copy in loads:
+        copy.wait()
+
+    a, b, x = g // 8, (g // 4) % 2, g % 4
+    base = d * 16 + x
+
+    def flag(offset, round_index):
+        return trades_ref[round_index, base + offset] == 1
+
+    far_mine, far_other = flag(b * 4, 0), flag((1 - b) * 4, 0)
+    near_mine, near_other = flag(a * 8, 1), flag((1 - a) * 8, 1)
+    near_at_source = jnp.logical_or(
+        jnp.logical_and(far_mine, near_other),
+        jnp.logical_and(jnp.logical_not(far_mine), near_mine),
+    )
+    far_at_source = jnp.logical_or(
+        jnp.logical_and(near_mine, far_other),
+        jnp.logical_and(jnp.logical_not(near_mine), far_mine),
+    )
 
     total_rows = count_ref[0] + 4
     key_bias = jnp.where(
@@ -241,7 +282,7 @@
             blend = term if blend is None else blend + term
         mixed_low = blend.astype(BF16)
         mixed[:, cols] = mixed_low
-        out = jnp.where(row_valid(), scale_ref[:, cols] * mixed_low.astype(F32), 0.0)
+        out = jnp.where(row_valid(), scale_ref[pl.ds(pair, 1), :] * mixed_low.astype(F32), 0.0)
         att[:, cols] = out.astype(BF16)
         return carry
 
@@ -256,7 +297,7 @@
 
     def backward(pair, carry):
         cols = columns(pair)
-        up = jnp.where(row_valid(), cot[:, cols].astype(F32) * scale_ref[:, cols], 0.0)
+        up = jnp.where(row_valid(), cot[:, cols].astype(F32) * scale_ref[pl.ds(pair, 1), :], 0.0)
         values = v[:, cols]
         blended = mixed[:, cols].astype(F32)
         dq_sum = dk_sum = dv_sum = None
@@ -269,15 +310,11 @@
             dq_sum = dq_term if j == 0 else dq_sum + dq_term
             dk_sum = dk_term if j == 0 else dk_sum + dk_term
             dv_sum = dv_term if j == 0 else dv_sum + dv_term
-        dq[:, cols] = (dq_sum * FACTOR).astype(BF16)
-        dk[:, cols] = (dk_sum * FACTOR).astype(BF16)
-        dv[:, cols] = dv_sum.astype(BF16)
+        dq[0, :, cols] = (dq_sum * FACTOR).astype(BF16)
+        dk[0, :, cols] = (dk_sum * FACTOR).astype(BF16)
+        dv[0, :, cols] = dv_sum.astype(BF16)
         return carry
 
-    for i in range(PARTS):
-        start(c_hop1[i])
-    for copy in loads:
-        copy.wait()
     lax.fori_loop(0, pairs // 2, forward, 0)
     c_turn(0)
     lax.fori_loop(pairs // 2, pairs, forward, 0)
@@ -291,66 +328,72 @@
     c_land(2)
     scale_part()
     sum_start(0)
-    lax.fori_loop(0, pairs // 2, backward, 0)
+    lax.fori_loop(0, 3, backward, 0)
+    sum_finish(0)
     a_turn(0)
-    sum_finish(0)
-    lax.fori_loop(pairs // 2, pairs, backward, 0)
-    grad_stores = [
-        pltpu.make_async_copy(src, dst.at[0], store_sem.at[i])
-        for i, (src, dst) in enumerate([(dq, dq_out), (dk, dk_out), (dv, dv_out)])
-    ]
-    for copy in grad_stores:
-        copy.start()
-    sum_finish(1)
+    lax.fori_loop(3, pairs, backward, 0)
+    for s in range(1, len(stages) - 1):
+        sum_finish(s)
     a_turn(1)
-    sum_finish(2)
     a_turn(2)
-    for s in range(3, len(stages)):
-        sum_finish(s)
+    sum_finish(len(stages) - 1)
     for i in range(PARTS):
         a_land(i)
-    for copy in grad_stores:
-        copy.wait()
     for i in range(PARTS):
         for hop in (c_hop1[i], c_hop2[i], a_hop1[i], a_hop2[i]):
             for copy in hop:
                 copy.wait_send()
-        a_store(i, 0).wait()
-        a_store(i, 1).wait()
     for s in range(len(stages)):
         for copy in sum_copies(s):
             copy.wait_send()
 
 
+def settle(*refs):
+    half = len(refs) // 2
+    sources, results, sem = refs[:half], refs[half:-1], refs[-1]
+    copies = [
+        pltpu.make_async_copy(src, dst, sem.at[i])
+        for i, (src, dst) in enumerate(zip(sources, results))
+    ]
+    for copy in copies:
+        copy.start()
+    for copy in copies:
+        copy.wait()
+
+
 def per_device(stages, query_rows, key_rows, value_rows, cotangent, kept_counts, trades, layer_scale):
     _, length, width = query_rows.shape
     heads = width // HEAD_DIM
-    image = jax.ShapeDtypeStruct(query_rows.shape, BF16)
+    tiles = width // LANES
     block = pltpu.VMEM((length, width), BF16)
+    image = pltpu.VMEM((1, length, width), BF16)
     hbm = pl.BlockSpec(memory_space=pl.ANY)
-    smem = pl.BlockSpec(memory_space=pltpu.SMEM)
     vmem = pl.BlockSpec(memory_space=pltpu.VMEM)
     slots = 8 * PARTS
-    attended, query_grad, key_grad, value_grad, scale_sum = pl.pallas_call(
+    meetings = sum(len(stage_moves(stage)) for stage in stages)
+    results = pl.pallas_call(
         functools.partial(kernel, stages),
-        out_shape=(image, image, image, image, jax.ShapeDtypeStruct((8, LANES), F32)),
-        in_specs=[hbm, hbm, hbm, hbm, smem, smem, vmem],
-        out_specs=(hbm, hbm, hbm, hbm, vmem),
+        out_shape=(image, image, image, image, pltpu.VMEM((tiles, LANES), F32)),
+        in_specs=[hbm] * 7,
+        out_specs=(vmem,) * 5,
         scratch_shapes=[
-            *[block] * 13,
+            *[block] * 12,
             pltpu.VMEM((heads, length, length), BF16),
-            *[block] * 4,
+            block,
             pltpu.VMEM((len(stages), 8, LANES), F32),
-            pltpu.VMEM((len(stages), 3, 8, LANES), F32),
-            pltpu.SemaphoreType.DMA((4,)),
-            pltpu.SemaphoreType.DMA((3 + 2 * PARTS,)),
+            pltpu.VMEM((len(stages), 7, 8, LANES), F32),
+            pltpu.VMEM((tiles, LANES), F32),
+            pltpu.SMEM((1,), jnp.int32),
+            pltpu.SMEM(trades.shape[::-1], jnp.int32),
+            pltpu.SemaphoreType.DMA((7,)),
             pltpu.SemaphoreType.DMA((slots,)),
             pltpu.SemaphoreType.DMA((slots,)),
-            pltpu.SemaphoreType.DMA((3 * len(stages),)),
-            pltpu.SemaphoreType.DMA((3 * len(stages),)),
+            pltpu.SemaphoreType.DMA((7 * len(stages),)),
+            pltpu.SemaphoreType.DMA((7 * len(stages),)),
+            pltpu.SemaphoreType.REGULAR((meetings,)),
         ],
         compiler_params=pltpu.CompilerParams(
-            collective_id=0, has_side_effects=True, vmem_limit_bytes=60 * 2**20
+            collective_id=0, has_side_effects=True, vmem_limit_bytes=52 * 2**20
         ),
         cost_estimate=pl.CostEstimate(
             flops=12 * heads * length * length * HEAD_DIM,
@@ -359,10 +402,17 @@
         ),
     )(
         query_rows, key_rows, value_rows, cotangent,
-        kept_counts, trades.T, layer_scale.reshape(1, width),
+        kept_counts, trades.T, layer_scale.reshape(tiles, LANES),
     )
-    scale_grad = scale_sum[: width // LANES].reshape(width)
-    return attended, query_grad, key_grad, value_grad, scale_grad
+    attended, query_grad, key_grad, value_grad, scale_sum = pl.pallas_call(
+        settle,
+        out_shape=tuple(jax.ShapeDtypeStruct(item.shape, item.dtype) for item in results),
+        in_specs=[hbm] * 5,
+        out_specs=(hbm,) * 5,
+        scratch_shapes=[pltpu.SemaphoreType.DMA((5,))],
+        compiler_params=pltpu.CompilerParams(vmem_limit_bytes=2**20),
+    )(*results)
+    return attended, query_grad, key_grad, value_grad, scale_sum.reshape(width)
 
 
 def solution(mesh):

time: 84.8 us -> 67 us (0.79)
  the two profiles are of different devices: /device:TPU:1 before, /device:TPU:64 now
where the time goes in v2:
time: 67 us; the launch traced here: 66.9 us
  Pallas kernels  65.6 us (98%)
  between operations  1.29 us (2%)
    pallas_call x1, Pallas kernels, per_device(): pl.pallas_call(functools.partial(kernel, stages), out_shape=(image, image...  64.2 us
    pallas_call x1, Pallas kernels, per_device(): pl.pallas_call(settle, out_shape=tuple((jax.ShapeDtypeStruct(item.shape,...  1.45 us

profile of v2, /device:TPU:64, one launch (start us, length us, event | category | flops | bytes accessed | tf_op | source)
XLA Modules:
  0.0 66.9 jit_solution(9969864508510257629)
XLA Ops:
  1.3 64.2 %shard_map.110 = (bf16[1,384,768]{2,1,0:T(8,128)(2,1)S(1)}, bf16[1,384,768]{2,1,0:T(8,128)(2,1)S(1)}, bf16[1,384,768]{2,1,0:T(8,128)(2,1)S(1)}, bf16[1,384,768]{2,1,0:T(8,128)(2,1)S(1)}, f32[6,128]{1,0:T(8,128)S(1)}) custom-call(bf16[1,384,768]{2,1,0:T(8,128)(2,1)} %q_hbm.1, bf16[1,384,768]{2,1,0:T(8,128)(2,1)} %k_hbm.1, bf16[1,384,768]{2,1,0:T(8,128)(2,1)} %v_hbm.1, ...), custom_call_target="tpu_custom_call" | custom-call | flops 1358954496 | bytes 4718592 | tf_op jit(solution)/shard_map/pallas_call | solution.py:374
  65.5 1.4 %shard_map.111 = (bf16[1,384,768]{2,1,0:T(8,128)(2,1)}, bf16[1,384,768]{2,1,0:T(8,128)(2,1)}, bf16[1,384,768]{2,1,0:T(8,128)(2,1)}, bf16[1,384,768]{2,1,0:T(8,128)(2,1)}, f32[6,128]{1,0:T(8,128)}) custom-call(bf16[1,384,768]{2,1,0:T(8,128)(2,1)S(1)} %get-tuple-element.15.refs_0_, bf16[1,384,768]{2,1,0:T(8,128)(2,1)S(1)} %get-tuple-element.16.refs_1_, ...), custom_call_target="tpu_custom_call" | custom-call | tf_op jit(solution)/shard_map/pallas_call | solution.py:407

commit v3 on v2

--- a/solution.py
+++ b/solution.py
@@ -15,7 +15,7 @@
 LANES = 128
 FACTOR = HEAD_DIM ** -0.5
 EXP_SCALE = FACTOR * math.log2(math.e)
-PARTS = 3
+PARTS = 4
 
 NEAR, FAR = 4, 8
 
@@ -43,7 +43,7 @@
         middle.insert(0, ("dp", bit))
         bit *= 2
     stages = [
-        [("group", 2), ("group", 1), ("dp", 1)], middle, [("dp", top), ("group", FAR), ("group", NEAR)]
+        [("dp", top), ("group", FAR), ("group", NEAR)], [("group", 2), ("group", 1), ("dp", 1)], middle
     ]
     return [stage for stage in stages if stage]
 
@@ -81,9 +81,17 @@
                 pd = flip(pd, bit)
         return (pd, pg)
 
+    def rank(pd, pg):
+        size = 2 ** sum(axis == "dp" for stage in stages for axis, _ in stage)
+        ny = size // 4
+        z, x = pd // (size // 2) * 4 + pg // 4, pg % 4
+        y, core = (pd // 2) % ny, pd % 2
+        y = jnp.where(2 * y < ny, y, ny // 2 + ny - 1 - y)
+        place = 2 * (((z * ny + y) * 4 + x) * 2 + 1 - core)
+        return jnp.where(pd + pg == 0, 64 * ny - 1, place)
+
     def upper(moves):
-        axis, bit = moves[0]
-        return ((g if axis == "group" else d) // bit) % 2
+        return rank(d, g) > rank(*peer(moves))
 
     loads = [
         pltpu.make_async_copy(src, dst, load_sem.at[i])
@@ -92,16 +100,15 @@
             (count_hbm, count_ref), (trades_hbm, trades_ref), (scale_hbm, scale_ref),
         ])
     ]
-    for copy in loads:
-        copy.start()
 
     meetings = [moves for stage in stages for moves in stage_moves(stage)]
+    meetings.sort(key=lambda moves: moves not in ([("group", NEAR)], [("group", FAR)]))
     barrier = pltpu.get_barrier_semaphore()
     greetings = 0
     for moves in meetings:
-        greetings = greetings + upper(moves)
-
-        @pl.when(upper(moves) == 0)
+        greetings = greetings + upper(moves).astype(jnp.int32)
+
+        @pl.when(jnp.logical_not(upper(moves)))
         def _(moves=moves):
             pl.semaphore_signal(barrier, inc=1, device_id=peer(moves), device_id_type=MESH)
 
@@ -111,7 +118,7 @@
 
     for j, moves in enumerate(meetings):
 
-        @pl.when(upper(moves) == 1)
+        @pl.when(upper(moves))
         def _(j=j, moves=moves):
             pl.semaphore_signal(ready.at[j], inc=1, device_id=peer(moves), device_id_type=MESH)
 
@@ -123,7 +130,7 @@
             return
         met.append(j)
 
-        @pl.when(upper(moves) == 0)
+        @pl.when(jnp.logical_not(upper(moves)))
         def _():
             pl.semaphore_wait(ready.at[j], 1)
 
@@ -223,12 +230,14 @@
         else:
             sum_out[...] = terms[0][: width // LANES]
 
-    start_near = [c_hop1[i][0] for i in range(PARTS)]
-    start_far = [c_hop1[i][1] for i in range(PARTS)]
     meet([("group", NEAR)])
-    start(start_near)
+    c_hop1[0][0].start()
     meet([("group", FAR)])
-    start(start_far)
+    c_hop1[0][1].start()
+    for i in range(1, PARTS):
+        start(c_hop1[i])
+    for copy in loads:
+        copy.start()
     for copy in loads:
         copy.wait()
 
@@ -286,13 +295,14 @@
         att[:, cols] = out.astype(BF16)
         return carry
 
-    def scale_part():
-        part[0] = jnp.zeros((8, LANES), F32)
+    def scale_rows(begin):
+        valid = begin + lax.broadcasted_iota(jnp.int32, (rows, LANES), 0) < total_rows
         for pair in range(pairs):
             cols = pl.ds(pair * LANES, LANES)
-            product = cot[:, cols].astype(F32) * mixed[:, cols].astype(F32)
-            part[0, pl.ds(pair, 1), :] = jnp.sum(
-                jnp.where(row_valid(), product, 0.0), axis=0, keepdims=True
+            span = pl.ds(begin, rows)
+            product = cot[span, cols].astype(F32) * mixed[span, cols].astype(F32)
+            part[0, pl.ds(pair, 1), :] += jnp.sum(
+                jnp.where(valid, product, 0.0), axis=0, keepdims=True
             )
 
     def backward(pair, carry):
@@ -318,27 +328,28 @@
     lax.fori_loop(0, pairs // 2, forward, 0)
     c_turn(0)
     lax.fori_loop(pairs // 2, pairs, forward, 0)
-    c_turn(1)
-    c_turn(2)
+    for i in range(1, PARTS):
+        c_turn(i)
     start(a_hop1[0])
-    c_land(0)
-    start(a_hop1[1])
-    c_land(1)
-    start(a_hop1[2])
-    c_land(2)
-    scale_part()
+    part[0] = jnp.zeros((8, LANES), F32)
+    for i in range(PARTS):
+        c_land(i)
+        scale_rows(i * rows)
+        scale_rows(half + i * rows)
     sum_start(0)
-    lax.fori_loop(0, 3, backward, 0)
-    sum_finish(0)
+    for i in range(1, PARTS):
+        start(a_hop1[i])
+    lax.fori_loop(0, pairs // 2, backward, 0)
     a_turn(0)
-    lax.fori_loop(3, pairs, backward, 0)
-    for s in range(1, len(stages) - 1):
+    lax.fori_loop(pairs // 2, pairs, backward, 0)
+    for i in range(1, PARTS):
+        a_turn(i)
+    for s in range(len(stages) - 1):
         sum_finish(s)
-    a_turn(1)
-    a_turn(2)
+    for i in range(PARTS - 1):
+        a_land(i)
     sum_finish(len(stages) - 1)
-    for i in range(PARTS):
-        a_land(i)
+    a_land(PARTS - 1)
     for i in range(PARTS):
         for hop in (c_hop1[i], c_hop2[i], a_hop1[i], a_hop2[i]):
             for copy in hop:

time: 67 us -> 66.2 us (0.988)
  the two profiles are of different devices: /device:TPU:64 before, /device:TPU:1 now
where the time goes in v3:
time: 66.2 us; the launch traced here: 66 us
  Pallas kernels  64.7 us (98%)
  between operations  1.29 us (2%)
    pallas_call x1, Pallas kernels, per_device(): pl.pallas_call(functools.partial(kernel, stages), out_shape=(image, image...  63.3 us
    pallas_call x1, Pallas kernels, per_device(): pl.pallas_call(settle, out_shape=tuple((jax.ShapeDtypeStruct(item.shape,...  1.45 us

profile of v3, /device:TPU:1, one launch (start us, length us, event | category | flops | bytes accessed | tf_op | source)
XLA Modules:
  0.0 66.0 jit_solution(11919747308570172821)
XLA Ops:
  1.3 63.3 %shard_map.110 = (bf16[1,384,768]{2,1,0:T(8,128)(2,1)S(1)}, bf16[1,384,768]{2,1,0:T(8,128)(2,1)S(1)}, bf16[1,384,768]{2,1,0:T(8,128)(2,1)S(1)}, bf16[1,384,768]{2,1,0:T(8,128)(2,1)S(1)}, f32[6,128]{1,0:T(8,128)S(1)}) custom-call(bf16[1,384,768]{2,1,0:T(8,128)(2,1)} %q_hbm.1, bf16[1,384,768]{2,1,0:T(8,128)(2,1)} %k_hbm.1, bf16[1,384,768]{2,1,0:T(8,128)(2,1)} %v_hbm.1, ...), custom_call_target="tpu_custom_call" | custom-call | flops 1358954496 | bytes 4718592 | tf_op jit(solution)/shard_map/pallas_call | solution.py:385
  64.6 1.4 %shard_map.111 = (bf16[1,384,768]{2,1,0:T(8,128)(2,1)}, bf16[1,384,768]{2,1,0:T(8,128)(2,1)}, bf16[1,384,768]{2,1,0:T(8,128)(2,1)}, bf16[1,384,768]{2,1,0:T(8,128)(2,1)}, f32[6,128]{1,0:T(8,128)}) custom-call(bf16[1,384,768]{2,1,0:T(8,128)(2,1)S(1)} %get-tuple-element.15.refs_0_, bf16[1,384,768]{2,1,0:T(8,128)(2,1)S(1)} %get-tuple-element.16.refs_1_, ...), custom_call_target="tpu_custom_call" | custom-call | tf_op jit(solution)/shard_map/pallas_call | solution.py:418

commit v4 on v3

--- a/solution.py
+++ b/solution.py
@@ -80,6 +80,10 @@
             else:
                 pd = flip(pd, bit)
         return (pd, pg)
+
+    def upper_half(move):
+        axis, bit = move
+        return ((g if axis == "group" else d) // bit) % 2 == 1
 
     def rank(pd, pg):
         size = 2 ** sum(axis == "dp" for stage in stages for axis, _ in stage)
@@ -330,15 +334,26 @@
     lax.fori_loop(pairs // 2, pairs, forward, 0)
     for i in range(1, PARTS):
         c_turn(i)
+    late = jnp.logical_or(upper_half(stages[0][0]), upper_half(("group", FAR)))
     start(a_hop1[0])
+
+    @pl.when(jnp.logical_not(late))
+    def _():
+        for i in range(1, PARTS):
+            start(a_hop1[i])
+
     part[0] = jnp.zeros((8, LANES), F32)
     for i in range(PARTS):
         c_land(i)
         scale_rows(i * rows)
         scale_rows(half + i * rows)
     sum_start(0)
-    for i in range(1, PARTS):
-        start(a_hop1[i])
+
+    @pl.when(late)
+    def _():
+        for i in range(1, PARTS):
+            start(a_hop1[i])
+
     lax.fori_loop(0, pairs // 2, backward, 0)
     a_turn(0)
     lax.fori_loop(pairs // 2, pairs, backward, 0)

time: 66.2 us -> 65.6 us (level)
  no operation moved by 1% of the time
where the time goes in v4:
time: 65.6 us; the launch traced here: 65.5 us
  Pallas kernels  64.2 us (98%)
  between operations  1.29 us (2%)
    pallas_call x1, Pallas kernels, per_device(): pl.pallas_call(functools.partial(kernel, stages), out_shape=(image, image...  62.7 us
    pallas_call x1, Pallas kernels, per_device(): pl.pallas_call(settle, out_shape=tuple((jax.ShapeDtypeStruct(item.shape,...  1.45 us

profile of v4, /device:TPU:1, one launch (start us, length us, event | category | flops | bytes accessed | tf_op | source)
XLA Modules:
  0.0 65.5 jit_solution(1283738293432048931)
XLA Ops:
  1.3 62.7 %shard_map.110 = (bf16[1,384,768]{2,1,0:T(8,128)(2,1)S(1)}, bf16[1,384,768]{2,1,0:T(8,128)(2,1)S(1)}, bf16[1,384,768]{2,1,0:T(8,128)(2,1)S(1)}, bf16[1,384,768]{2,1,0:T(8,128)(2,1)S(1)}, f32[6,128]{1,0:T(8,128)S(1)}) custom-call(bf16[1,384,768]{2,1,0:T(8,128)(2,1)} %q_hbm.1, bf16[1,384,768]{2,1,0:T(8,128)(2,1)} %k_hbm.1, bf16[1,384,768]{2,1,0:T(8,128)(2,1)} %v_hbm.1, ...), custom_call_target="tpu_custom_call" | custom-call | flops 1358954496 | bytes 4718592 | tf_op jit(solution)/shard_map/pallas_call | solution.py:400
  64.0 1.4 %shard_map.111 = (bf16[1,384,768]{2,1,0:T(8,128)(2,1)}, bf16[1,384,768]{2,1,0:T(8,128)(2,1)}, bf16[1,384,768]{2,1,0:T(8,128)(2,1)}, bf16[1,384,768]{2,1,0:T(8,128)(2,1)}, f32[6,128]{1,0:T(8,128)}) custom-call(bf16[1,384,768]{2,1,0:T(8,128)(2,1)S(1)} %get-tuple-element.15.refs_0_, bf16[1,384,768]{2,1,0:T(8,128)(2,1)S(1)} %get-tuple-element.16.refs_1_, ...), custom_call_target="tpu_custom_call" | custom-call | tf_op jit(solution)/shard_map/pallas_call | solution.py:433

commit v5 on v4

--- a/solution.py
+++ b/solution.py
@@ -120,12 +120,15 @@
     def _():
         pl.semaphore_wait(barrier, greetings)
 
-    for j, moves in enumerate(meetings):
-
-        @pl.when(upper(moves))
-        def _(j=j, moves=moves):
-            pl.semaphore_signal(ready.at[j], inc=1, device_id=peer(moves), device_id_type=MESH)
-
+    def answer(j):
+        @pl.when(upper(meetings[j]))
+        def _():
+            pl.semaphore_signal(
+                ready.at[j], inc=1, device_id=peer(meetings[j]), device_id_type=MESH
+            )
+
+    answer(0)
+    answer(1)
     met = []
 
     def meet(moves):
@@ -242,6 +245,8 @@
         start(c_hop1[i])
     for copy in loads:
         copy.start()
+    for j in range(2, len(meetings)):
+        answer(j)
     for copy in loads:
         copy.wait()
 
@@ -364,14 +369,15 @@
     for i in range(PARTS - 1):
         a_land(i)
     sum_finish(len(stages) - 1)
+
+    sent = [copy for i in range(PARTS) for hop in (c_hop1[i], c_hop2[i], a_hop1[i]) for copy in hop]
+    sent += [copy for s in range(len(stages)) for copy in sum_copies(s)]
+    sent += [copy for hop in a_hop2[:-1] for copy in hop]
+    for copy in sent:
+        copy.wait_send()
     a_land(PARTS - 1)
-    for i in range(PARTS):
-        for hop in (c_hop1[i], c_hop2[i], a_hop1[i], a_hop2[i]):
-            for copy in hop:
-                copy.wait_send()
-    for s in range(len(stages)):
-        for copy in sum_copies(s):
-            copy.wait_send()
+    for copy in a_hop2[-1]:
+        copy.wait_send()
 
 
 def settle(*refs):

time: 65.6 us -> 65.6 us (level)
  no operation moved by 1% of the time
where the time goes in v5:
time: 65.6 us; the launch traced here: 65.4 us
  Pallas kernels  64.1 us (98%)
  between operations  1.29 us (2%)
    pallas_call x1, Pallas kernels, per_device(): pl.pallas_call(functools.partial(kernel, stages), out_shape=(image, image...  62.7 us
    pallas_call x1, Pallas kernels, per_device(): pl.pallas_call(settle, out_shape=tuple((jax.ShapeDtypeStruct(item.shape,...  1.45 us

profile of v5, /device:TPU:1, one launch (start us, length us, event | category | flops | bytes accessed | tf_op | source)
XLA Modules:
  0.0 65.4 jit_solution(14636145161692526211)
XLA Ops:
  1.3 62.7 %shard_map.110 = (bf16[1,384,768]{2,1,0:T(8,128)(2,1)S(1)}, bf16[1,384,768]{2,1,0:T(8,128)(2,1)S(1)}, bf16[1,384,768]{2,1,0:T(8,128)(2,1)S(1)}, bf16[1,384,768]{2,1,0:T(8,128)(2,1)S(1)}, f32[6,128]{1,0:T(8,128)S(1)}) custom-call(bf16[1,384,768]{2,1,0:T(8,128)(2,1)} %q_hbm.1, bf16[1,384,768]{2,1,0:T(8,128)(2,1)} %k_hbm.1, bf16[1,384,768]{2,1,0:T(8,128)(2,1)} %v_hbm.1, ...), custom_call_target="tpu_custom_call" | custom-call | flops 1358954496 | bytes 4718592 | tf_op jit(solution)/shard_map/pallas_call | solution.py:406
  64.0 1.4 %shard_map.111 = (bf16[1,384,768]{2,1,0:T(8,128)(2,1)}, bf16[1,384,768]{2,1,0:T(8,128)(2,1)}, bf16[1,384,768]{2,1,0:T(8,128)(2,1)}, bf16[1,384,768]{2,1,0:T(8,128)(2,1)}, f32[6,128]{1,0:T(8,128)}) custom-call(bf16[1,384,768]{2,1,0:T(8,128)(2,1)S(1)} %get-tuple-element.15.refs_0_, bf16[1,384,768]{2,1,0:T(8,128)(2,1)S(1)} %get-tuple-element.16.refs_1_, ...), custom_call_target="tpu_custom_call" | custom-call | tf_op jit(solution)/shard_map/pallas_call | solution.py:439
